TPU v7x, 32 devices: a whole 2x2x4 slice. The times are simulated.
32 devices in a mesh: head: 4 (over z), vocab: 8 (over y, x, core).
Axes of the slice: x: 2, y: 2, z: 4, core: 2. Of those that a mesh axis runs over, the one named last changes fastest.
Arguments:
- hidden_states: bfloat16 [256, 8192], P(('head', 'vocab')), may hold values from -6 to 6
- head_weight: bfloat16 [4, 8192, 16384], P('head', None, 'vocab'), may hold values from -1 to 1
- tags: int32 [256, 1], P(('head', 'vocab')), may hold values from 0 to 3; in each aligned block of 8 rows (0 to 7, 8 to 15, ...) at most 2 rows name the same one
- targets: int32 [256], P(('head', 'vocab')), may hold values from 0 to 16383
- row_grad: bfloat16 [256], P(('head', 'vocab')), may hold values from -192 to 192
Outputs:
- row_loss: bfloat16 [256], P(('head', 'vocab'))
- hidden_grad: bfloat16 [256, 8192], P(('head', 'vocab'))
Inputs may be any that keep to these rules, and one draw needn't show every extreme that they name: `tags`: in each aligned block of 8 rows (the rows of one device) no head is named by more than 2 rows, and in every draw some block has exactly 2 rows of one head.
All inputs are finite; a program needn't handle non-finite values.
Results may differ from a plain program's by a relative error of at most 0.018.
Values may be sent and summed in bfloat16 or wider, within the bound.
A program may use at most 64 MiB of HBM per device.

v0:
```python
import jax
import jax.numpy as jnp
from jax import lax
from jax.sharding import PartitionSpec as P

CAP = 2


def project_back(dlog_block, weight):
    return lax.dot_general(
        dlog_block, weight, (((1,), (1,)), ((), ())), preferred_element_type=jnp.float32
    )


def per_device(hidden_states, head_weight, tags, targets, row_grad):
    head_count = lax.axis_size("head")
    own_rows = head_count * CAP
    row_tag = tags[:, 0]
    local_rows = row_tag.shape[0]
    row_iota = lax.broadcasted_iota(jnp.int32, (local_rows, local_rows), 0)
    col_iota = lax.broadcasted_iota(jnp.int32, (local_rows, local_rows), 1)
    earlier = (row_tag[None, :] == row_tag[:, None]) & (col_iota < row_iota)
    slot_rank = jnp.sum(earlier.astype(jnp.int32), axis=1)
    slot_index = row_tag * CAP + slot_rank
    selector = jnp.arange(own_rows, dtype=jnp.int32)[:, None] == slot_index[None, :]
    send_rows = jnp.dot(
        selector.astype(jnp.bfloat16), hidden_states, preferred_element_type=jnp.float32
    ).astype(jnp.bfloat16)
    send_rows = send_rows.reshape(head_count, CAP, hidden_states.shape[1])
    send_targets = jnp.sum(jnp.where(selector, targets[None, :], 0), axis=1).reshape(
        head_count, CAP
    )
    send_scale = (
        jnp.sum(jnp.where(selector, row_grad[None, :].astype(jnp.float32), 0.0), axis=1)
        .astype(jnp.bfloat16)
        .reshape(head_count, CAP)
    )
    arrived = (
        lax.all_to_all(send_rows, "head", split_axis=0, concat_axis=0, tiled=True),
        lax.all_to_all(send_targets, "head", split_axis=0, concat_axis=0, tiled=True),
        lax.all_to_all(send_scale, "head", split_axis=0, concat_axis=0, tiled=True),
    )
    grouped = (
        lax.all_gather(arrived[0], "vocab", axis=0, tiled=True),
        lax.all_gather(arrived[1], "vocab", axis=0, tiled=True),
        lax.all_gather(arrived[2], "vocab", axis=0, tiled=True),
    )
    gathered = grouped[0].reshape(-1, hidden_states.shape[1])
    group_targets = grouped[1].reshape(-1)
    group_scale = grouped[2].reshape(-1).astype(jnp.float32)
    weight = head_weight[0]
    vocab_width = weight.shape[1]
    logits = jnp.dot(gathered, weight, preferred_element_type=jnp.float32)
    offset = lax.axis_index("vocab") * vocab_width
    target_hit = lax.broadcasted_iota(jnp.int32, logits.shape, 1) + offset == group_targets[:, None]
    own_target = jnp.sum(jnp.where(target_hit, logits, 0.0), axis=1)
    row_top = lax.pmax(jnp.max(logits, axis=1), "vocab")
    local_total = jnp.sum(jnp.exp(logits - row_top[:, None]), axis=1)
    row_total, target_logit = lax.psum((local_total, own_target), "vocab")
    group_loss = (jnp.log(row_total) + row_top - target_logit).astype(jnp.bfloat16)
    probabilities = jnp.exp(logits - row_top[:, None]) / row_total[:, None]
    dlogits = (group_scale[:, None] * (probabilities - target_hit.astype(jnp.float32))).astype(
        jnp.bfloat16
    )
    partial_value = project_back(dlogits, weight)
    summed = lax.psum(partial_value.astype(jnp.bfloat16), "vocab").astype(jnp.float32)
    own_grad = lax.dynamic_slice_in_dim(summed, lax.axis_index("vocab") * own_rows, own_rows, 0)
    own_loss = lax.dynamic_slice_in_dim(group_loss, lax.axis_index("vocab") * own_rows, own_rows, 0)
    returned = (
        lax.all_to_all(
            own_grad.astype(jnp.bfloat16).reshape(head_count, CAP, -1),
            "head",
            split_axis=0,
            concat_axis=0,
            tiled=True,
        ),
        lax.all_to_all(
            own_loss.reshape(head_count, CAP), "head", split_axis=0, concat_axis=0, tiled=True
        ),
    )
    back_grad = returned[0].reshape(own_rows, -1)
    back_loss = returned[1].reshape(1, own_rows).astype(jnp.float32)
    hidden_grad = jnp.dot(
        selector.T.astype(jnp.bfloat16), back_grad, preferred_element_type=jnp.float32
    ).astype(jnp.bfloat16)
    row_loss = jnp.sum(jnp.where(selector.T, back_loss, 0.0), axis=1).astype(jnp.bfloat16)
    return (row_loss, hidden_grad)


def solution(mesh):
    placed = (
        P(("head", "vocab"), None),
        P("head", None, "vocab"),
        P(("head", "vocab"), None),
        P(("head", "vocab")),
        P(("head", "vocab")),
    )
    return jax.shard_map(
        per_device,
        mesh=mesh,
        in_specs=placed,
        out_specs=(P(("head", "vocab")), P(("head", "vocab"), None)),
        check_vma=False,
    )
```

profile of v0, /device:TPU:0, one launch (start us, length us, event | category | flops | bytes accessed | tf_op | source)
XLA Modules:
  0.0 201.5 jit_solution(13037015004279756340)
XLA Ops:
  7.2 0.9 convert_reduce_fusion.1
  8.1 0.7 multiply_add_fusion
  8.8 0.2 convolution_convert_fusion.1
  9.0 0.1 reshape.73
  9.1 12.3 %all_to_all.41 = bf16[4,2,8192]{2,1,0:T(2,128)(2,1)} all-to-all(bf16[4,2,8192]{2,1,0:T(2,128)(2,1)S(1)} %reshape.73), channel_id=1, replica_groups=mesh['head'=4,'vocab'=8] {'head'}, dimensions={0} | all-to-all | bytes 262144 | tf_op jit(solution)/shard_map/all_to_all | solution.py:39
  21.4 0.8 select_reduce_fusion.2
  22.2 0.7 all_to_all.27
  22.8 3.2 %all-to-all-start.1 = ((s32[4,1,2]{2,1,0:T(1,128)}), s32[4,1,2]{2,1,0:T(1,128)S(1)}, u32[]{:S(2)}, u32[]{:S(2)}) async-start(s32[4,1,2]{2,1,0:T(1,128)} %bitcast.2), calls=%async_computation.1 | async-start | bytes 4096 | tf_op jit(solution)/shard_map/all_to_all | solution.py:40
  26.1 0.7 convert_element_type.77
  26.8 4.7 %all-to-all-done.1 = s32[4,1,2]{2,1,0:T(1,128)S(1)} async-done(((s32[4,1,2]{2,1,0:T(1,128)}), s32[4,1,2]{2,1,0:T(1,128)S(1)}, u32[]{:S(2)}, u32[]{:S(2)}) %all-to-all-start.1) | async-done | bytes 64 | tf_op jit(solution)/shard_map/all_to_all | solution.py:40
  31.5 8.9 %all-gather = s32[32,1,2]{2,1,0:T(1,128)S(1)} all-gather(s32[4,1,2]{2,1,0:T(1,128)S(1)} %all-to-all-done.1), channel_id=2, replica_groups=mesh['head'=4,'vocab'=8] {'vocab'}, dimensions={0}, use_global_device_ids=true | all-gather | bytes 288 | tf_op jit(solution)/shard_map/all_gather | solution.py:45
  40.4 0.5 broadcast.26
  40.9 0.7 reduce.11
  41.6 0.1 eq.52
  41.7 2.4 %all-gather.4.cloned.1.call-done = bf16[32,2,8192]{2,1,0:T(2,128)(2,1)} async-done(((bf16[4,2,8192]{2,1,0:T(2,128)(2,1)}), bf16[32,2,8192]{2,1,0:T(2,128)(2,1)}) %all-gather.4.cloned.1.call-update) | async-done | bytes 1048592 | tf_op jit(solution)/shard_map/all_gather | solution.py:44
  44.1 1.5 reshape.74
  45.6 13.7 %fusion.21 = (f32[64]{0:T(128)S(1)}, f32[64,2048]{1,0:T(8,128)S(1)}) fusion(bf16[64,8192]{1,0:T(8,128)(2,1)S(1)} %reshape.74, bf16[1,8192,2048]{2,1,0:T(8,128)(2,1)} %param.6), kind=kOutput, calls=%fused_computation.36 | convolution fusion | flops 2147614720 | bytes 35127552 | tf_op jit(solution)/shard_map/dot_general | solution.py:53
  59.4 13.1 %pmax.7 = f32[64]{0:T(128)S(1)} all-reduce(f32[64]{0:T(128)S(1)} %get-tuple-element.8), channel_id=1, replica_groups=mesh['head'=4,'vocab'=8] {'vocab'}, use_global_device_ids=true, to_apply=%region_2.3 | all-reduce | flops 64 | bytes 512 | tf_op jit(solution)/shard_map/pmax | solution.py:57
  72.5 0.3 fusion.11
  72.8 11.8 %all-reduce = (f32[64]{0:T(128)S(1)}, f32[64]{0:T(128)S(1)}) all-reduce(f32[64]{0:T(128)S(1)} %get-tuple-element.3, f32[64]{0:T(128)S(1)} %get-tuple-element.2), channel_id=1, replica_groups=mesh['head'=4,'vocab'=8] {'vocab'}, use_global_device_ids=true, to_apply=%region_7.8 | all-reduce | flops 128 | bytes 1024 | tf_op jit(solution)/shard_map/psum | solution.py:59
  84.7 0.1 all_to_all.35
  84.7 9.9 %all_to_all.42 = bf16[4,1,2]{2,1,0:T(2,128)(2,1)S(1)} all-to-all(bf16[4,1,2]{2,1,0:T(2,128)(2,1)S(1)} %all_to_all.35), channel_id=1, replica_groups=mesh['head'=4,'vocab'=8] {'head'}, dimensions={0} | all-to-all | bytes 32 | tf_op jit(solution)/shard_map/all_to_all | solution.py:77
  94.8 0.7 select_reduce_fusion
  95.6 7.9 %all_to_all.43 = bf16[4,1,2]{2,1,0:T(2,128)(2,1)S(1)} all-to-all(bf16[4,1,2]{2,1,0:T(2,128)(2,1)S(1)} %convert_element_type.91), channel_id=1, replica_groups=mesh['head'=4,'vocab'=8] {'head'}, dimensions={0} | all-to-all | bytes 32 | tf_op jit(solution)/shard_map/all_to_all | solution.py:41
  103.4 8.8 %all-gather.1 = bf16[32,1,2]{2,1,0:T(2,128)(2,1)S(1)} all-gather(bf16[4,1,2]{2,1,0:T(2,128)(2,1)S(1)} %all_to_all.43), channel_id=3, replica_groups=mesh['head'=4,'vocab'=8] {'vocab'}, dimensions={0}, use_global_device_ids=true | all-gather | bytes 144 | tf_op jit(solution)/shard_map/all_gather | solution.py:46
  112.3 0.1 reshape.78
  112.5 16.0 %fusion.4 = bf16[64,8192]{1,0:T(8,128)(2,1)} fusion(bf16[1,8192,2048]{2,1,0:T(8,128)(2,1)} %param.6, f32[64,2048]{1,0:T(8,128)S(1)} %get-tuple-element.9, f32[64]{0:T(128)S(1)} %get-tuple-element.7, f32[64]{0:T(128)S(1)} %reshape.78, s32[2048]{0:T(1024)S(1)} %iota_add_fusion, f32[64]{0:T(128)S(1)} %pmax.7, s32[64]{0:T(128)S(1)} %eq.52), kind=kOutput, calls=%fused_computation.4 | convolution fusion | flops 2148925440 | bytes 35136512 | tf_op jit(solution)/shard_map/dot_general | solution.py:10
  128.5 54.0 %all-reduce.3.cloned.1.call-done = bf16[64,8192]{1,0:T(8,128)(2,1)} async-done(((bf16[64,8192]{1,0:T(8,128)(2,1)}), bf16[64,8192]{1,0:T(8,128)(2,1)}) %all-reduce.3.cloned.1.call-update) | async-done | bytes 1048592 | tf_op jit(solution)/shard_map/psum | solution.py:66
  182.6 0.9 convert_convert_fusion
  183.5 0.1 reshape.75
  183.6 10.2 %all_to_all.44 = bf16[4,2,8192]{2,1,0:T(2,128)(2,1)S(1)} all-to-all(bf16[4,2,8192]{2,1,0:T(2,128)(2,1)S(1)} %reshape.75), channel_id=1, replica_groups=mesh['head'=4,'vocab'=8] {'head'}, dimensions={0} | all-to-all | bytes 262144 | tf_op jit(solution)/shard_map/all_to_all | solution.py:70
  193.8 0.9 convolution_convert_fusion
  (14 shorter events, 0.5 us)
Async XLA Ops:
  7.2 1.6 copy-start
  7.2 37.0 %all-gather.4.cloned.1.call-start = ((), (), s32[]{:S(2)}) async-start(), calls=%async_computation.5 | async-start | bytes 1179648 | tf_op jit(solution)/shard_map/all_gather | solution.py:44
  22.8 8.7 %all-to-all-start.1 = ((s32[4,1,2]{2,1,0:T(1,128)}), s32[4,1,2]{2,1,0:T(1,128)S(1)}, u32[]{:S(2)}, u32[]{:S(2)}) async-start(s32[4,1,2]{2,1,0:T(1,128)} %bitcast.2), calls=%async_computation.1 | async-start | bytes 4096 | tf_op jit(solution)/shard_map/all_to_all | solution.py:40
  26.1 156.5 %all-reduce.3.cloned.1.call-start = ((), (), s32[]{:S(2)}) async-start(), calls=%async_computation.6 | async-start | bytes 2097152 | tf_op jit(solution)/shard_map/psum | solution.py:66
Sparse Core Ops, SparseCore 0:
  21.5 22.5 all-gather.3
  128.6 53.8 all-reduce.2
where the time goes:
time: 202 us
  blocking collectives  82.9 us (41%)
  waiting for transfers between devices  61.2 us (30%)
  matrix products  30.8 us (15%)
  between operations  14.1 us (7%)
  other arithmetic  5.68 us (3%)
  local copies, waits for them, and re-layouts  3.44 us (2%)
  starting transfers between devices  3.3 us (2%)
    psum x1, waiting for transfers between devices, per_device(): lax.psum(partial_value.astype(jnp.bfloat16), 'vocab').astype(jnp.float32)  54 us
    dot_general x1, matrix products, project_back(): lax.dot_general(dlog_block, weight, (((1,), (1,)), ((), ())), preferred_e...  16 us
    dot_general x1, matrix products, per_device(): logits = jnp.dot(gathered, weight, preferred_element_type=jnp.float32)  13.7 us
    pmax x1, blocking collectives, per_device(): row_top = lax.pmax(jnp.max(logits, axis=1), 'vocab')  13.1 us
    all_to_all x1, blocking collectives, per_device(): lax.all_to_all(send_rows, 'head', split_axis=0, concat_axis=0, tiled=True)  12.3 us
    psum x1, blocking collectives, per_device(): row_total, target_logit = lax.psum((local_total, own_target), 'vocab')  11.8 us
    all_to_all x1, blocking collectives, per_device(): lax.all_to_all(own_grad.astype(jnp.bfloat16).reshape(head_count, CAP, -1)...  10.2 us
    all_to_all x1, blocking collectives, per_device(): lax.all_to_all(own_loss.reshape(head_count, CAP), 'head', split_axis=0, c...  9.94 us
  transfers between devices with their start and end apart: 3, of which 3 were waited for; matrix products, arithmetic and copies ran while one was open for 1% of the time, Pallas kernels for 0%

commit v1 on v0

v1 whole, which is shorter than its diff:
```python
import functools

import jax
import jax.numpy as jnp
from jax import lax
from jax.experimental import pallas as pl
from jax.experimental.pallas import tpu as pltpu
from jax.sharding import PartitionSpec as P

CAP = 2
CHUNKS = 8
MESH = pl.DeviceIdType.MESH
F32 = jnp.float32
BF16 = jnp.bfloat16


def iota(shape, dim):
    return lax.broadcasted_iota(jnp.int32, shape, dim).astype(F32)


def transposed(vector, axis):
    n = max(vector.shape)
    eye = iota((n, n), 0) == iota((n, n), 1)
    return jnp.sum(jnp.where(eye, vector, 0.0), axis=axis, keepdims=True)


def kernel(
    n_head, n_vocab, chunks,
    meta_ref, hidden_ref, w_hbm, loss_ref, grad_ref,
    w_ref, row_out, row_in, rows, meta_out, meta_in, meta_all, logit_ref, dlog_ref,
    stat_all, part, pair_out, pair_in, sum_out, sum_in, back_out, back_in, loss_out, loss_in,
    w_sem, row_s, row_r, meta_s, meta_r, spread_s, spread_r, share_s, share_r,
    all_s, all_r, stat_s, stat_r, pair_s, pair_r, sum_s, sum_r, back_s, back_r, loss_s, loss_r,
):
    my_head, my_vocab = lax.axis_index("head"), lax.axis_index("vocab")
    n_chip = n_vocab // 2
    chip, core = my_vocab // 2, my_vocab % 2
    own = n_head * CAP
    local, depth = hidden_ref.shape
    width = depth // chunks
    group = n_vocab * own
    columns = w_ref.shape[1]

    def span(k):
        return pl.ds(pl.multiple_of(k * width, width), width)

    def load_weight(k):
        part_k = pl.ds(pl.multiple_of(k * width, width), width)
        return pltpu.make_async_copy(w_hbm.at[0, part_k], w_ref.at[part_k], w_sem.at[k])

    for k in range(chunks):
        load_weight(k).start()

    def head_peer(d):
        return ((my_head + d) % n_head, my_vocab)

    def vocab_peer(d):
        return (my_head, (my_vocab + d) % n_vocab)

    def chip_peer(d):
        return (my_head, ((chip + d) % n_chip) * 2 + core)

    def place(v):
        return (v % 2) * n_chip + v // 2

    partner = (my_head, chip * 2 + 1 - core)
    my_place = place(my_vocab)

    def remote(src, dst, send, recv, device):
        return pltpu.make_async_remote_copy(
            src_ref=src, dst_ref=dst, send_sem=send, recv_sem=recv,
            device_id=device, device_id_type=MESH,
        )

    def send_row(d, k):
        return remote(row_out.at[d, :, span(k)], row_in.at[d, :, span(k)],
                      row_s.at[d, k], row_r.at[d, k], head_peer(d))

    def send_meta(d):
        return remote(meta_out.at[d], meta_in.at[d], meta_s.at[d], meta_r.at[d], head_peer(d))

    def spread(d, k, slot):
        return remote(rows.at[slot, :, span(k)], rows.at[slot, :, span(k)],
                      spread_s.at[d, k], spread_r.at[d, k], chip_peer(d))

    def share(d, k, slot):
        return remote(rows.at[slot, :, span(k)], rows.at[slot, :, span(k)],
                      share_s.at[d, k], share_r.at[d, k], partner)

    def send_all(d, slot):
        return remote(meta_all.at[slot], meta_all.at[slot], all_s.at[d], all_r.at[d], vocab_peer(d))

    def send_stat(d, slot):
        return remote(stat_all.at[slot], stat_all.at[slot], stat_s.at[d], stat_r.at[d], vocab_peer(d))

    def send_pair(k):
        return remote(pair_out.at[:, :, span(k)], pair_in.at[:, :, span(k)],
                      pair_s.at[k], pair_r.at[k], partner)

    def send_sum(d, k):
        return remote(sum_out.at[d, :, span(k)], sum_in.at[d, :, span(k)],
                      sum_s.at[d, k], sum_r.at[d, k], chip_peer(d))

    def send_back(d, k):
        return remote(back_out.at[d, :, span(k)], back_in.at[d, :, span(k)],
                      back_s.at[d, k], back_r.at[d, k], head_peer(d))

    def send_loss(d):
        return remote(loss_out, loss_in.at[d], loss_s.at[d], loss_r.at[d], head_peer(d))

    barrier = pltpu.get_barrier_semaphore()
    for d in range(1, n_head):
        pl.semaphore_signal(barrier, inc=1, device_id=head_peer(d), device_id_type=MESH)
    for d in range(1, n_vocab):
        pl.semaphore_signal(barrier, inc=1, device_id=vocab_peer(d), device_id_type=MESH)

    tag_row = meta_ref[0:1, :]
    target_row = meta_ref[1:2, :]
    scale_row = meta_ref[2:3, :]
    tag_col = transposed(tag_row, 1)
    earlier = (tag_col == tag_row) & (iota((local, local), 0) < iota((local, local), 1))
    rank_row = jnp.sum(jnp.where(earlier, 1.0, 0.0), axis=0, keepdims=True)
    slot_row = tag_row * CAP + rank_row
    slot_col = transposed(slot_row, 1)
    home = my_head.astype(F32)

    def head_at(d):
        return ((my_head + d + n_head) % n_head).astype(F32)

    lane = iota((own, 128), 1)
    meta_tiles = []
    for d in range(n_head):
        seat = iota((own, local), 0) - home * CAP
        mask = (slot_row == head_at(d) * CAP + seat) & (seat >= 0) & (seat < CAP)
        goal = jnp.sum(jnp.where(mask, target_row, 0.0), axis=1, keepdims=True)
        scale = jnp.sum(jnp.where(mask, scale_row, 0.0), axis=1, keepdims=True)
        tile = jnp.where(lane == 0, goal, jnp.where(lane == 1, scale, 0.0))
        (meta_in if d == 0 else meta_out)[d] = tile
    for d in range(n_head):
        chosen = jnp.where(slot_row == head_at(d) * CAP + iota((CAP, local), 0), 1.0, 0.0)
        picked = jnp.dot(chosen.astype(BF16), hidden_ref[...], preferred_element_type=F32)
        (row_in if d == 0 else row_out)[d] = picked.astype(BF16)

    pl.semaphore_wait(barrier, n_head + n_vocab - 2)

    for d in range(1, n_head):
        send_meta(d).start()

    def start_rows(k, carry):
        for d in range(1, n_head):
            send_row(d, k).start()
        return carry

    lax.fori_loop(0, chunks, start_rows, 0)

    def gather_rows(k, carry):
        total = jnp.zeros((own, width), F32)
        for d in range(n_head):
            if d:
                send_row(d, k).wait_recv()
            put = jnp.where(
                iota((own, CAP), 0) == head_at(-d) * CAP + iota((own, CAP), 1), 1.0, 0.0
            )
            total += jnp.dot(put.astype(BF16), row_in[d, :, span(k)], preferred_element_type=F32)
        rows[my_place, :, span(k)] = total.astype(BF16)
        for d in range(1, n_chip):
            spread(d, k, my_place).start()
        share(0, k, my_place).start()
        return carry

    lax.fori_loop(0, chunks, gather_rows, 0)

    tile = meta_in[0]
    for d in range(1, n_head):
        send_meta(d).wait_recv()
        tile += meta_in[d]
    meta_all[my_place] = tile
    for d in range(1, n_vocab):
        send_all(d, my_place).start()

    logit_ref[...] = jnp.zeros_like(logit_ref)

    def forward_share(k):
        for d in range(1, n_chip):
            slot = core * n_chip + (chip - d + n_chip) % n_chip
            spread(d, k, slot).wait_recv()
            share(d, k, slot).start()

    forward_share(0)

    def multiply(k, carry):
        @pl.when(k + 1 < chunks)
        def _():
            forward_share(k + 1)

        for d in range(n_chip):
            slot = (1 - core) * n_chip + (chip - d + n_chip) % n_chip
            share(d, k, slot).wait_recv()
        load_weight(k).wait()
        x = rows[:, :, span(k)].reshape(group, width)
        logit_ref[...] += jnp.dot(x, w_ref[span(k), :], preferred_element_type=F32)
        return carry

    lax.fori_loop(0, chunks, multiply, 0)

    for d in range(1, n_vocab):
        send_all(d, place((my_vocab - d + n_vocab) % n_vocab)).wait_recv()
    info = meta_all[...].reshape(group, 128)
    goal_col = info[:, 0:1] - (my_vocab * columns).astype(F32)
    scale_col = info[:, 1:2]
    logits = logit_ref[...]
    hit = iota((group, columns), 1) == goal_col
    top_col = jnp.max(logits, axis=1, keepdims=True)
    target_col = jnp.sum(jnp.where(hit, logits, 0.0), axis=1, keepdims=True)
    grown = jnp.exp(logits - top_col)
    logit_ref[...] = grown
    total_col = jnp.sum(grown, axis=1, keepdims=True)
    line = iota((8, group), 0)
    stat_all[my_place] = jnp.where(
        line == 0, transposed(top_col, 0),
        jnp.where(line == 1, transposed(total_col, 0), transposed(target_col, 0)),
    )
    for d in range(1, n_vocab):
        send_stat(d, my_place).start()
    for d in range(1, n_vocab):
        send_stat(d, place((my_vocab - d + n_vocab) % n_vocab)).wait_recv()
    tops = stat_all[:, 0, :]
    row_top = jnp.max(tops, axis=0, keepdims=True)
    row_total = jnp.sum(stat_all[:, 1, :] * jnp.exp(tops - row_top), axis=0, keepdims=True)
    row_target = jnp.sum(stat_all[:, 2, :], axis=0, keepdims=True)
    loss_row = jnp.log(row_total) + row_top - row_target
    mine = iota((own, group), 1) == iota((own, group), 0) + (my_place * own).astype(F32)
    loss_col = jnp.sum(jnp.where(mine, loss_row, 0.0), axis=1, keepdims=True)
    loss_out[...] = jnp.broadcast_to(loss_col, (own, 128))
    for d in range(1, n_head):
        send_loss(d).start()
    factor_col = scale_col * jnp.exp(top_col - transposed(row_top, 1)) / transposed(row_total, 1)
    hit = iota((group, columns), 1) == goal_col
    dlog_ref[...] = (logit_ref[...] * factor_col - jnp.where(hit, scale_col, 0.0)).astype(BF16)

    def back(k, carry):
        @pl.when(k < chunks)
        def _():
            value = lax.dot_general(
                dlog_ref[...], w_ref[span(k), :], (((1,), (1,)), ((), ())),
                preferred_element_type=F32,
            )
            part[k % 2] = value.reshape(2, n_chip, own, width)
            pair_out[:, :, span(k)] = part[k % 2, 1 - core].astype(BF16)
            send_pair(k).start()

        @pl.when((k >= 1) & (k < chunks + 1))
        def _():
            j = k - 1
            send_pair(j).wait_recv()
            for d in range(1, n_chip):
                to = (chip + d) % n_chip
                both = part[j % 2, core, to] + pair_in[to, :, span(j)].astype(F32)
                sum_out[d, :, span(j)] = both.astype(BF16)
                send_sum(d, j).start()
            both = part[j % 2, core, chip] + pair_in[chip, :, span(j)].astype(F32)
            sum_in[0, :, span(j)] = both.astype(BF16)

        @pl.when(k >= 2)
        def _():
            j = k - 2
            total = sum_in[0, :, span(j)].astype(F32)
            for d in range(1, n_chip):
                send_sum(d, j).wait_recv()
                total += sum_in[d, :, span(j)].astype(F32)
            total = total.astype(BF16)
            for d in range(n_head):
                take = jnp.where(
                    iota((CAP, own), 1) == head_at(d) * CAP + iota((CAP, own), 0), 1.0, 0.0
                )
                piece = jnp.dot(take.astype(BF16), total, preferred_element_type=F32)
                (back_out if d else back_in)[d, :, span(j)] = piece.astype(BF16)
                if d:
                    send_back(d, j).start()

        return carry

    lax.fori_loop(0, chunks + 2, back, 0)

    loss = jnp.zeros((1, local), F32)
    for d in range(n_head):
        if d:
            send_loss(d).wait_recv()
            tile = loss_in[d]
        else:
            tile = loss_out[...]
        mask = (tag_row == head_at(-d)) & (iota((own, local), 0) == home * CAP + rank_row)
        loss += jnp.sum(jnp.where(mask, tile[:, :local], 0.0), axis=0, keepdims=True)
    loss_ref[...] = loss

    def finish(k, carry):
        total = jnp.zeros((local, width), F32)
        for d in range(n_head):
            if d:
                send_back(d, k).wait_recv()
            put = jnp.where(slot_col == head_at(-d) * CAP + iota((local, CAP), 1), 1.0, 0.0)
            total += jnp.dot(put.astype(BF16), back_in[d, :, span(k)], preferred_element_type=F32)
        grad_ref[:, span(k)] = total.astype(BF16)
        return carry

    lax.fori_loop(0, chunks, finish, 0)

    def drain(k, carry):
        for d in range(1, n_head):
            send_row(d, k).wait_send()
            send_back(d, k).wait_send()
        for d in range(1, n_chip):
            spread(d, k, my_place).wait_send()
            send_sum(d, k).wait_send()
        for d in range(n_chip):
            share(d, k, core * n_chip + (chip - d + n_chip) % n_chip).wait_send()
        send_pair(k).wait_send()
        return carry

    lax.fori_loop(0, chunks, drain, 0)
    for d in range(1, n_head):
        send_meta(d).wait_send()
        send_loss(d).wait_send()
    for d in range(1, n_vocab):
        send_all(d, my_place).wait_send()
        send_stat(d, my_place).wait_send()


def per_device(n_head, n_vocab, hidden_states, head_weight, tags, targets, row_grad):
    local, depth = hidden_states.shape
    columns = head_weight.shape[2]
    own = n_head * CAP
    n_chip = n_vocab // 2
    group = n_vocab * own
    chunks = CHUNKS
    width = depth // chunks
    meta = jnp.stack([tags[:, 0].astype(F32), targets.astype(F32), row_grad.astype(F32)])
    vmem = pl.BlockSpec(memory_space=pltpu.VMEM)
    dma = pltpu.SemaphoreType.DMA
    loss, grad = pl.pallas_call(
        functools.partial(kernel, n_head, n_vocab, chunks),
        out_shape=(
            jax.ShapeDtypeStruct((1, local), F32),
            jax.ShapeDtypeStruct((local, depth), BF16),
        ),
        in_specs=[vmem, vmem, pl.BlockSpec(memory_space=pl.ANY)],
        out_specs=(vmem, vmem),
        scratch_shapes=[
            pltpu.VMEM((depth, columns), BF16),
            pltpu.VMEM((n_head, CAP, depth), BF16),
            pltpu.VMEM((n_head, CAP, depth), BF16),
            pltpu.VMEM((n_vocab, own, depth), BF16),
            pltpu.VMEM((n_head, own, 128), F32),
            pltpu.VMEM((n_head, own, 128), F32),
            pltpu.VMEM((n_vocab, own, 128), F32),
            pltpu.VMEM((group, columns), F32),
            pltpu.VMEM((group, columns), BF16),
            pltpu.VMEM((n_vocab, 8, group), F32),
            pltpu.VMEM((2, 2, n_chip, own, width), F32),
            pltpu.VMEM((n_chip, own, depth), BF16),
            pltpu.VMEM((n_chip, own, depth), BF16),
            pltpu.VMEM((n_chip, own, depth), BF16),
            pltpu.VMEM((n_chip, own, depth), BF16),
            pltpu.VMEM((n_head, CAP, depth), BF16),
            pltpu.VMEM((n_head, CAP, depth), BF16),
            pltpu.VMEM((own, 128), F32),
            pltpu.VMEM((n_head, own, 128), F32),
            dma((chunks,)),
            dma((n_head, chunks)), dma((n_head, chunks)),
            dma((n_head,)), dma((n_head,)),
            dma((n_chip, chunks)), dma((n_chip, chunks)),
            dma((n_chip, chunks)), dma((n_chip, chunks)),
            dma((n_vocab,)), dma((n_vocab,)),
            dma((n_vocab,)), dma((n_vocab,)),
            dma((chunks,)), dma((chunks,)),
            dma((n_chip, chunks)), dma((n_chip, chunks)),
            dma((n_head, chunks)), dma((n_head, chunks)),
            dma((n_head,)), dma((n_head,)),
        ],
        compiler_params=pltpu.CompilerParams(
            collective_id=0, has_side_effects=True, vmem_limit_bytes=56 * 1024 * 1024
        ),
    )(meta, hidden_states, head_weight)
    return loss[0].astype(BF16), grad


def solution(mesh):
    placed = (
        P(("head", "vocab"), None),
        P("head", None, "vocab"),
        P(("head", "vocab"), None),
        P(("head", "vocab")),
        P(("head", "vocab")),
    )
    return jax.shard_map(
        functools.partial(per_device, mesh.shape["head"], mesh.shape["vocab"]),
        mesh=mesh,
        in_specs=placed,
        out_specs=(P(("head", "vocab")), P(("head", "vocab"), None)),
        check_vma=False,
    )
```

time: 202 us -> 61.2 us (0.30)
  blocking collectives: 82.9 us -> 0 us
  waiting for transfers between devices: 61.2 us -> 0 us
  Pallas kernels: 0 us -> 55.1 us
  matrix products: 30.8 us -> 0 us
  between operations: 14.1 us -> 0.64 us
  starting transfers between devices: 3.3 us -> 0 us
    pallas_call x0 -> x1, Pallas kernels: none -> 55.1 us  [per_device(): pl.pallas_call(functools.partial(kernel, n_head, n_vocab, chunks), out_sh...]
    psum x1 -> x0, waiting for transfers between devices: 54 us -> none  [per_device(): lax.psum(partial_value.astype(jnp.bfloat16), 'vocab').astype(jnp.float32)]
    all_to_all x4 -> x0, blocking collectives: 40.3 us -> none  [the longest x1 12.3 us: per_device(): lax.all_to_all(send_rows, 'head', split_axis=0, concat_axis=0, tiled=True)]
    dot_general x4 -> x0, matrix products: 30.8 us -> none  [the longest x1 16 us: project_back(): lax.dot_general(dlog_block, weight, (((1,), (1,)), ((), ())), preferred_e...]
    all_gather x2 -> x0, blocking collectives: 17.7 us -> none  [the longest x1 8.88 us: per_device(): lax.all_gather(arrived[1], 'vocab', axis=0, tiled=True)]
    pmax x1 -> x0, blocking collectives: 13.1 us -> none  [per_device(): row_top = lax.pmax(jnp.max(logits, axis=1), 'vocab')]
    psum x1 -> x0, blocking collectives: 11.8 us -> none  [per_device(): row_total, target_logit = lax.psum((local_total, own_target), 'vocab')]
    all_to_all x1 -> x0, waiting for transfers between devices: 4.73 us -> none  [per_device(): lax.all_to_all(send_targets, 'head', split_axis=0, concat_axis=0, tiled=T...]
  transfers between devices with their start and end apart: 3 -> 0, of which waited for: 3 -> 0; matrix products, arithmetic and copies ran while one was open for 1% -> 0% of each run, Pallas kernels for 0% -> 0%
where the time goes in v1:
time: 61.2 us; the launch traced here: 61 us
  Pallas kernels  55.1 us (90%)
  other arithmetic  3.74 us (6%)
  local copies, waits for them, and re-layouts  1.57 us (3%)
  between operations  0.64 us (1%)
    pallas_call x1, Pallas kernels, per_device(): pl.pallas_call(functools.partial(kernel, n_head, n_vocab, chunks), out_sh...  55.1 us
    another operation x3, other arithmetic, per_device(): jnp.stack([tags[:, 0].astype(F32), targets.astype(F32), row_grad.astype(F...  1.9 us
    unnamed x1, local copies, waits for them, and re-layouts  1.57 us

profile of v1, /device:TPU:0, one launch (start us, length us, event | category | flops | bytes accessed | tf_op | source)
XLA Modules:
  0.0 61.0 jit_solution(16585304841499078282)
XLA Ops:
  0.6 0.7 %convert_bitcast_fusion.2 = f32[1,8]{1,0:T(1,128)S(1)} fusion(s32[8,1]{0,1:T(1,128)} %param.7), kind=kLoop, calls=%fused_computation.4 | loop fusion | flops 8 | bytes 64 | tf_op jit(solution)/shard_map/convert_element_type | solution.py:337
  1.3 0.7 %convert_bitcast_fusion.1 = f32[1,8]{1,0:T(1,128)S(1)} fusion(s32[8]{0:T(128)} %param.8), kind=kLoop, calls=%fused_computation.3 | loop fusion | flops 8 | bytes 64 | tf_op jit(solution)/shard_map/stack | solution.py:337
  1.9 0.7 %bitcast_convert_fusion = f32[1,8]{1,0:T(1,128)S(1)} fusion(bf16[8]{0:T(256)(128)(2,1)} %param.9), kind=kLoop, calls=%fused_computation.1 | loop fusion | flops 8 | bytes 48 | tf_op jit(solution)/shard_map/stack | solution.py:337
  2.6 0.6 pad_maximum_fusion.meta_ref
  3.2 55.1 %shard_map.68 = (f32[1,8]{1,0:T(1,128)}, bf16[8,8192]{1,0:T(8,128)(2,1)}) custom-call(f32[3,8]{1,0:T(4,128)} %pad_maximum_fusion.meta_ref, bf16[8,8192]{1,0:T(8,128)(2,1)} %hidden_ref.1, bf16[1,8192,2048]{2,1,0:T(8,128)(2,1)} %w_hbm.1), custom_call_target="tpu_custom_call" | custom-call | tf_op jit(solution)/shard_map/pallas_call | solution.py:340
  58.3 1.2 %convert_bitcast_fusion = bf16[8]{0:T(256)(128)(2,1)} fusion(f32[1,8]{1,0:T(1,128)} %get-tuple-element.4), kind=kLoop, calls=%fused_computation.2 | loop fusion | flops 8 | bytes 48 | tf_op jit(solution)/shard_map/convert_element_type | solution.py:384
  59.5 1.6 %copy.8 = bf16[8,8192]{1,0:T(8,128)(2,1)} copy(bf16[8,8192]{1,0:T(8,128)(2,1)} %get-tuple-element.9) | data formatting | bytes 262144

commit v2 on v1

v2 whole, which is shorter than its diff:
```python
import functools

import jax
import jax.numpy as jnp
from jax import lax
from jax.experimental import pallas as pl
from jax.experimental.pallas import tpu as pltpu
from jax.sharding import PartitionSpec as P

CAP = 2
CHUNKS = 8
BATCHES = 4
MESH = pl.DeviceIdType.MESH
F32 = jnp.float32
BF16 = jnp.bfloat16


def iota(shape, dim):
    return lax.broadcasted_iota(jnp.int32, shape, dim).astype(F32)


def transposed(vector, axis):
    n = max(vector.shape)
    eye = iota((n, n), 0) == iota((n, n), 1)
    return jnp.sum(jnp.where(eye, vector, 0.0), axis=axis, keepdims=True)


def kernel(
    n_head, n_vocab, chunks, batches,
    tag_ref, target_ref, scale_ref, hidden_ref, w_hbm, loss_ref, grad_ref,
    w_ref, stage, row_out, row_in, rows, meta_out, meta_in, meta_all, logit_ref, dlog_ref,
    stat_all, part, pair_out, pair_in, sum_out, sum_in, back_out, back_in, loss_out, loss_in,
    w_sem, row_s, row_r, meta_s, meta_r, spread_s, spread_r, share_s, share_r,
    all_s, all_r, stat_s, stat_r, pair_s, pair_r, sum_s, sum_r, back_s, back_r, loss_s, loss_r,
):
    my_head, my_vocab = lax.axis_index("head"), lax.axis_index("vocab")
    n_chip = n_vocab // 2
    chip, core = my_vocab // 2, my_vocab % 2
    own = n_head * CAP
    local, depth = hidden_ref.shape
    width = depth // chunks
    wide = depth // batches
    group = n_vocab * own
    columns = w_ref.shape[1]

    def span(k):
        return pl.ds(pl.multiple_of(k * width, width), width)

    def wide_span(k):
        return pl.ds(pl.multiple_of(k * wide, wide), wide)

    def load_weight(k):
        return pltpu.make_async_copy(w_hbm.at[0, span(k)], w_ref.at[span(k)], w_sem.at[k])

    for k in range(chunks):
        load_weight(k).start()

    def head_peer(d):
        return ((my_head + d + n_head) % n_head, my_vocab)

    def vocab_peer(d):
        return (my_head, (my_vocab + d) % n_vocab)

    def chip_peer(d):
        return (my_head, ((chip + d) % n_chip) * 2 + core)

    partner = (my_head, chip * 2 + 1 - core)
    my_place = core * n_chip + chip

    def remote(src, dst, send, recv, device):
        return pltpu.make_async_remote_copy(
            src_ref=src, dst_ref=dst, send_sem=send, recv_sem=recv,
            device_id=device, device_id_type=MESH,
        )

    def whole(ref, count, send, recv, cut=None):
        view = ref.at[pl.ds(0, count)] if cut is None else ref.at[pl.ds(0, count), :, cut]
        return remote(view, view, send, recv, partner)

    barrier = pltpu.get_barrier_semaphore()
    for d in range(1, n_head):
        pl.semaphore_signal(barrier, inc=1, device_id=head_peer(d), device_id_type=MESH)
    for d in range(1, n_vocab):
        pl.semaphore_signal(barrier, inc=1, device_id=vocab_peer(d), device_id_type=MESH)

    tag_col = tag_ref[...].astype(F32)
    tag_row = transposed(tag_col, 0)
    target_row = target_ref[...].astype(F32)
    scale_row = scale_ref[...].astype(F32)
    earlier = (tag_col == tag_row) & (iota((local, local), 0) < iota((local, local), 1))
    rank_row = jnp.sum(jnp.where(earlier, 1.0, 0.0), axis=0, keepdims=True)
    slot_row = tag_row * CAP + rank_row
    slot_col = transposed(slot_row, 1)
    home = my_head.astype(F32)

    def wanted(seat):
        distance = jnp.floor(seat * (1.0 / CAP))
        head = home + distance
        head = jnp.where(head >= n_head, head - n_head, head)
        return head * CAP + seat - distance * CAP

    full = slot_row == wanted(iota((own, local), 0))
    picked = jnp.dot(
        jnp.where(full, 1.0, 0.0).astype(BF16), hidden_ref[...], preferred_element_type=F32
    )
    stage[...] = picked
    for d in range(n_head):
        piece = stage[d * CAP : (d + 1) * CAP, :].astype(BF16)
        (row_out if d else row_in)[d] = piece
    goal = jnp.sum(jnp.where(full, target_row, 0.0), axis=1, keepdims=True)
    scale = jnp.sum(jnp.where(full, scale_row, 0.0), axis=1, keepdims=True)
    lane, line = iota((own, 128), 1), iota((own, 128), 0)
    tile = jnp.where(lane == 0, goal, jnp.where(lane == 1, scale, 0.0))
    for d in range(n_head):
        kept = jnp.where((line >= d * CAP) & (line < (d + 1) * CAP), tile, 0.0)
        (meta_out if d else meta_in)[d] = kept

    pl.semaphore_wait(barrier, n_head + n_vocab - 2)

    for k in range(batches):
        for d in range(1, n_head):
            remote(row_out.at[d, :, wide_span(k)], row_in.at[d, :, wide_span(k)],
                   row_s, row_r.at[k], head_peer(d)).start()
        if k == 0:
            for d in range(1, n_head):
                remote(meta_out.at[d], meta_in.at[d], meta_s, meta_r, head_peer(d)).start()

    def gather_rows(k, carry):
        cut = wide_span(k)
        whole(row_in, n_head - 1, row_s, row_r.at[k], cut).wait_recv()
        for d in range(n_head):
            stage[d * CAP : (d + 1) * CAP, cut] = row_in[d, :, cut].astype(F32)
        rows[my_place, :, cut] = stage[:, cut].astype(BF16)
        block = rows.at[my_place, :, cut]
        for d in range(1, n_chip):
            remote(block, block, spread_s, spread_r.at[k], chip_peer(d)).start()
        return carry

    lax.fori_loop(0, batches, gather_rows, 0)

    whole(meta_in, n_head - 1, meta_s, meta_r).wait_recv()
    meta_all[my_place] = jnp.sum(meta_in[...], axis=0)
    for d in range(1, n_vocab):
        remote(meta_all.at[my_place], meta_all.at[my_place], all_s, all_r, vocab_peer(d)).start()

    logit_ref[...] = jnp.zeros_like(logit_ref)

    def forward_share(k):
        cut = wide_span(k)
        whole(rows, n_chip - 1, spread_s, spread_r.at[k], cut).wait_recv()
        half = rows.at[pl.ds(core * n_chip, n_chip), :, cut]
        remote(half, half, share_s, share_r.at[k], partner).start()

    forward_share(0)

    def multiply(k, carry):
        @pl.when(k + 1 < batches)
        def _():
            forward_share(k + 1)

        whole(rows, n_chip, share_s, share_r.at[k], wide_span(k)).wait_recv()
        for i in range(chunks // batches):
            j = k * (chunks // batches) + i
            load_weight(j).wait()
            x = rows[:, :, span(j)].reshape(group, width)
            logit_ref[...] += jnp.dot(x, w_ref[span(j), :], preferred_element_type=F32)
        return carry

    lax.fori_loop(0, batches, multiply, 0)

    whole(meta_all, n_vocab - 1, all_s, all_r).wait_recv()
    info = meta_all[...].reshape(group, 128)
    goal_col = info[:, 0:1] - (my_vocab * columns).astype(F32)
    scale_col = info[:, 1:2]
    logits = logit_ref[...]
    hit = iota((group, columns), 1) == goal_col
    top_col = jnp.max(logits, axis=1, keepdims=True)
    target_col = jnp.sum(jnp.where(hit, logits, 0.0), axis=1, keepdims=True)
    grown = jnp.exp(logits - top_col)
    logit_ref[...] = grown
    total_col = jnp.sum(grown, axis=1, keepdims=True)
    line = iota((8, group), 0)
    stat_all[my_place] = jnp.where(
        line == 0, transposed(top_col, 0),
        jnp.where(line == 1, transposed(total_col, 0), transposed(target_col, 0)),
    )
    for d in range(1, n_vocab):
        remote(stat_all.at[my_place], stat_all.at[my_place], stat_s, stat_r, vocab_peer(d)).start()
    whole(stat_all, n_vocab - 1, stat_s, stat_r).wait_recv()
    tops = stat_all[:, 0, :]
    row_top = jnp.max(tops, axis=0, keepdims=True)
    row_total = jnp.sum(stat_all[:, 1, :] * jnp.exp(tops - row_top), axis=0, keepdims=True)
    factor_col = scale_col * jnp.exp(top_col - transposed(row_top, 1)) / transposed(row_total, 1)
    hit = iota((group, columns), 1) == goal_col
    dlog_ref[...] = (logit_ref[...] * factor_col - jnp.where(hit, scale_col, 0.0)).astype(BF16)

    row_target = jnp.sum(stat_all[:, 2, :], axis=0, keepdims=True)
    loss_row = jnp.log(row_total) + row_top - row_target
    mine = iota((own, group), 1) == iota((own, group), 0) + (my_place * own).astype(F32)
    loss_col = jnp.sum(jnp.where(mine, loss_row, 0.0), axis=1, keepdims=True)
    loss_out[...] = jnp.broadcast_to(loss_col, (own, 128))
    for d in range(1, n_head):
        remote(loss_out, loss_in.at[d], loss_s, loss_r, head_peer(-d)).start()

    give_back = slot_col == wanted(iota((local, own), 1))
    give_back = jnp.where(give_back, 1.0, 0.0).astype(BF16)

    def back(k, carry):
        @pl.when(k < chunks)
        def _():
            value = lax.dot_general(
                dlog_ref[...], w_ref[span(k), :], (((1,), (1,)), ((), ())),
                preferred_element_type=F32,
            )
            part[k % 2] = value.reshape(2, n_chip, own, width)
            pair_out[:, :, span(k)] = part[k % 2, 1 - core].astype(BF16)
            remote(pair_out.at[:, :, span(k)], pair_in.at[:, :, span(k)],
                   pair_s, pair_r.at[k], partner).start()

        @pl.when((k >= 1) & (k < chunks + 1))
        def _():
            j = k - 1
            whole(pair_in, n_chip, pair_s, pair_r.at[j], span(j)).wait_recv()
            for d in range(1, n_chip):
                to = (chip + d) % n_chip
                both = part[j % 2, core, to] + pair_in[to, :, span(j)].astype(F32)
                sum_out[d, :, span(j)] = both.astype(BF16)
                remote(sum_out.at[d, :, span(j)], sum_in.at[d, :, span(j)],
                       sum_s, sum_r.at[j], chip_peer(d)).start()
            both = part[j % 2, core, chip] + pair_in[chip, :, span(j)].astype(F32)
            sum_in[0, :, span(j)] = both.astype(BF16)

        @pl.when((k >= 2) & (k < chunks + 2))
        def _():
            j = k - 2
            whole(sum_in, n_chip - 1, sum_s, sum_r.at[j], span(j)).wait_recv()
            stage[:, span(j)] = jnp.sum(sum_in[:, :, span(j)].astype(F32), axis=0)
            for d in range(n_head):
                piece = stage[d * CAP : (d + 1) * CAP, span(j)].astype(BF16)
                (back_out if d else back_in)[d, :, span(j)] = piece
                if d:
                    remote(back_out.at[d, :, span(j)], back_in.at[d, :, span(j)],
                           back_s, back_r.at[j], head_peer(-d)).start()

        @pl.when(k >= 4)
        def _():
            j = k - 4
            whole(back_in, n_head - 1, back_s, back_r.at[j], span(j)).wait_recv()
            for d in range(n_head):
                stage[d * CAP : (d + 1) * CAP, span(j)] = back_in[d, :, span(j)].astype(F32)
            grad_ref[:, span(j)] = jnp.dot(
                give_back, stage[:, span(j)].astype(BF16), preferred_element_type=F32
            ).astype(BF16)

        return carry

    lax.fori_loop(0, chunks + 4, back, 0)

    whole(loss_in, n_head - 1, loss_s, loss_r).wait_recv()
    loss = jnp.zeros((1, local), F32)
    for d in range(n_head):
        tile = loss_in[d] if d else loss_out[...]
        there = home + d
        there = jnp.where(there >= n_head, there - n_head, there)
        mask = (tag_row == there) & (iota((own, local), 0) == d * CAP + rank_row)
        loss += jnp.sum(jnp.where(mask, tile[:, :local], 0.0), axis=0, keepdims=True)
    loss_ref[...] = loss.astype(BF16)

    whole(row_out, n_head - 1, row_s, row_r.at[0]).wait_send()
    whole(back_out, n_head - 1, back_s, back_r.at[0]).wait_send()
    whole(meta_out, n_head - 1, meta_s, meta_r).wait_send()
    whole(loss_in, n_head - 1, loss_s, loss_r).wait_send()
    whole(rows, n_chip - 1, spread_s, spread_r.at[0]).wait_send()
    whole(rows, n_chip, share_s, share_r.at[0]).wait_send()
    whole(pair_out, n_chip, pair_s, pair_r.at[0]).wait_send()
    whole(sum_out, n_chip - 1, sum_s, sum_r.at[0]).wait_send()
    whole(meta_all, n_vocab - 1, all_s, all_r).wait_send()
    whole(stat_all, n_vocab - 1, stat_s, stat_r).wait_send()


def per_device(n_head, n_vocab, hidden_states, head_weight, tags, targets, row_grad):
    local, depth = hidden_states.shape
    columns = head_weight.shape[2]
    own = n_head * CAP
    n_chip = n_vocab // 2
    group = n_vocab * own
    chunks = CHUNKS
    width = depth // chunks
    vmem = pl.BlockSpec(memory_space=pltpu.VMEM)
    dma = pltpu.SemaphoreType.DMA
    loss, grad = pl.pallas_call(
        functools.partial(kernel, n_head, n_vocab, chunks, BATCHES),
        out_shape=(
            jax.ShapeDtypeStruct((1, local), BF16),
            jax.ShapeDtypeStruct((local, depth), BF16),
        ),
        in_specs=[vmem, vmem, vmem, vmem, pl.BlockSpec(memory_space=pl.ANY)],
        out_specs=(vmem, vmem),
        scratch_shapes=[
            pltpu.VMEM((depth, columns), BF16),
            pltpu.VMEM((own, depth), F32),
            pltpu.VMEM((n_head, CAP, depth), BF16),
            pltpu.VMEM((n_head, CAP, depth), BF16),
            pltpu.VMEM((n_vocab, own, depth), BF16),
            pltpu.VMEM((n_head, own, 128), F32),
            pltpu.VMEM((n_head, own, 128), F32),
            pltpu.VMEM((n_vocab, own, 128), F32),
            pltpu.VMEM((group, columns), F32),
            pltpu.VMEM((group, columns), BF16),
            pltpu.VMEM((n_vocab, 8, group), F32),
            pltpu.VMEM((2, 2, n_chip, own, width), F32),
            pltpu.VMEM((n_chip, own, depth), BF16),
            pltpu.VMEM((n_chip, own, depth), BF16),
            pltpu.VMEM((n_chip, own, depth), BF16),
            pltpu.VMEM((n_chip, own, depth), BF16),
            pltpu.VMEM((n_head, CAP, depth), BF16),
            pltpu.VMEM((n_head, CAP, depth), BF16),
            pltpu.VMEM((own, 128), F32),
            pltpu.VMEM((n_head, own, 128), F32),
            dma((chunks,)),
            dma, dma((BATCHES,)),
            dma, dma,
            dma, dma((BATCHES,)),
            dma, dma((BATCHES,)),
            dma, dma,
            dma, dma,
            dma, dma((chunks,)),
            dma, dma((chunks,)),
            dma, dma((chunks,)),
            dma, dma,
        ],
        compiler_params=pltpu.CompilerParams(
            collective_id=0, has_side_effects=True, vmem_limit_bytes=56 * 1024 * 1024
        ),
    )(tags, targets.reshape(1, local), row_grad.reshape(1, local), hidden_states, head_weight)
    return loss.reshape(local), grad


def solution(mesh):
    placed = (
        P(("head", "vocab"), None),
        P("head", None, "vocab"),
        P(("head", "vocab"), None),
        P(("head", "vocab")),
        P(("head", "vocab")),
    )
    return jax.shard_map(
        functools.partial(per_device, mesh.shape["head"], mesh.shape["vocab"]),
        mesh=mesh,
        in_specs=placed,
        out_specs=(P(("head", "vocab")), P(("head", "vocab"), None)),
        check_vma=False,
    )
```

time: 61.2 us -> 56.3 us (0.920)
  other arithmetic: 3.74 us -> 0 us
  Pallas kernels: 55.1 us -> 51.4 us
  local copies, waits for them, and re-layouts: 1.57 us -> 4.07 us
    pallas_call x1, Pallas kernels: 55.1 us -> 51.4 us  [per_device(): pl.pallas_call(functools.partial(kernel, n_head, n_vocab, chunks, BATCHES...]
    unnamed x1 -> x3, local copies, waits for them, and re-layouts: 1.57 us -> 4.07 us
    another operation x3 -> x0, other arithmetic: 1.9 us -> none  [per_device(): jnp.stack([tags[:, 0].astype(F32), targets.astype(F32), row_grad.astype(F...]
    convert_element_type x2 -> x0, other arithmetic: 1.84 us -> none  [the longest x1 1.18 us: per_device(): return (loss[0].astype(BF16), grad)]
where the time goes in v2:
time: 56.3 us; the launch traced here: 56.1 us
  Pallas kernels  51.4 us (91%)
  local copies, waits for them, and re-layouts  4.07 us (7%)
  between operations  0.64 us (1%)
    pallas_call x1, Pallas kernels, per_device(): pl.pallas_call(functools.partial(kernel, n_head, n_vocab, chunks, BATCHES...  51.4 us
    unnamed x3, local copies, waits for them, and re-layouts  4.07 us

profile of v2, /device:TPU:0, one launch (start us, length us, event | category | flops | bytes accessed | tf_op | source)
XLA Modules:
  0.0 56.1 jit_solution(5709196620191697390)
XLA Ops:
  0.6 1.3 %copy.7.tag_ref = s32[8,1]{1,0:T(8,128)} copy(s32[8,1]{0,1:T(1,128)} %param.7) | data formatting | bytes 64 | tf_op args[2]
  2.0 51.4 %shard_map.68 = (bf16[1,8]{1,0:T(2,128)(2,1)}, bf16[8,8192]{1,0:T(8,128)(2,1)}) custom-call(s32[8,1]{1,0:T(8,128)} %copy.7.tag_ref, s32[1,8]{1,0:T(1,128)} %bitcast.3, bf16[1,8]{1,0:T(2,128)(2,1)} %bitcast.4, bf16[8,8192]{1,0:T(8,128)(2,1)} %hidden_ref.1, bf16[1,8192,2048]{2,1,0:T(8,128)(2,1)} %w_hbm.1), custom_call_target="tpu_custom_call" | custom-call | tf_op jit(solution)/shard_map/pallas_call | solution.py:291
  53.4 1.2 %copy.10 = bf16[8]{0:T(256)(128)(2,1)} copy(bf16[8]{0:T(256)(128)(2,1)} %bitcast.5) | data formatting | bytes 32
  54.5 1.6 %copy.11 = bf16[8,8192]{1,0:T(8,128)(2,1)} copy(bf16[8,8192]{1,0:T(8,128)(2,1)} %get-tuple-element.9) | data formatting | bytes 262144

commit v3 on v2

--- a/solution.py
+++ b/solution.py
@@ -83,8 +83,8 @@
     for d in range(1, n_vocab):
         pl.semaphore_signal(barrier, inc=1, device_id=vocab_peer(d), device_id_type=MESH)
 
-    tag_col = tag_ref[...].astype(F32)
-    tag_row = transposed(tag_col, 0)
+    tag_row = tag_ref[...].astype(F32)
+    tag_col = transposed(tag_row, 1)
     target_row = target_ref[...].astype(F32)
     scale_row = scale_ref[...].astype(F32)
     earlier = (tag_col == tag_row) & (iota((local, local), 0) < iota((local, local), 1))
@@ -209,10 +209,10 @@
         @pl.when(k < chunks)
         def _():
             value = lax.dot_general(
-                dlog_ref[...], w_ref[span(k), :], (((1,), (1,)), ((), ())),
+                w_ref[span(k), :], dlog_ref[...], (((1,), (1,)), ((), ())),
                 preferred_element_type=F32,
             )
-            part[k % 2] = value.reshape(2, n_chip, own, width)
+            part[k % 2] = value.T.reshape(2, n_chip, own, width)
             pair_out[:, :, span(k)] = part[k % 2, 1 - core].astype(BF16)
             remote(pair_out.at[:, :, span(k)], pair_in.at[:, :, span(k)],
                    pair_s, pair_r.at[k], partner).start()
@@ -276,6 +276,11 @@
     whole(sum_out, n_chip - 1, sum_s, sum_r.at[0]).wait_send()
     whole(meta_all, n_vocab - 1, all_s, all_r).wait_send()
     whole(stat_all, n_vocab - 1, stat_s, stat_r).wait_send()
+
+
+def hand_over(loss_in, grad_in, loss_ref, grad_ref):
+    loss_ref[...] = loss_in[...]
+    grad_ref[...] = grad_in[...]
 
 
 def per_device(n_head, n_vocab, hidden_states, head_weight, tags, targets, row_grad):
@@ -332,7 +337,16 @@
         compiler_params=pltpu.CompilerParams(
             collective_id=0, has_side_effects=True, vmem_limit_bytes=56 * 1024 * 1024
         ),
-    )(tags, targets.reshape(1, local), row_grad.reshape(1, local), hidden_states, head_weight)
+    )(tags.reshape(1, local), targets.reshape(1, local), row_grad.reshape(1, local), hidden_states, head_weight)
+    loss, grad = pl.pallas_call(
+        hand_over,
+        out_shape=(
+            jax.ShapeDtypeStruct((1, local), BF16),
+            jax.ShapeDtypeStruct((local, depth), BF16),
+        ),
+        in_specs=[vmem, vmem],
+        out_specs=(vmem, vmem),
+    )(loss, grad)
     return loss.reshape(local), grad
 
 

time: 56.3 us -> 53.2 us (0.945)
  local copies, waits for them, and re-layouts: 4.07 us -> 0 us
  Pallas kernels: 51.4 us -> 52.5 us
    unnamed x3 -> x0, local copies, waits for them, and re-layouts: 4.07 us -> none
    pallas_call x0 -> x1, Pallas kernels: none -> 1.58 us  [per_device(): pl.pallas_call(hand_over, out_shape=(jax.ShapeDtypeStruct((1, local), BF1...]
where the time goes in v3:
time: 53.2 us; the launch traced here: 53.1 us
  Pallas kernels  52.5 us (99%)
  between operations  0.64 us (1%)
    pallas_call x1, Pallas kernels, per_device(): pl.pallas_call(functools.partial(kernel, n_head, n_vocab, chunks, BATCHES...  50.9 us
    pallas_call x1, Pallas kernels, per_device(): pl.pallas_call(hand_over, out_shape=(jax.ShapeDtypeStruct((1, local), BF1...  1.58 us

profile of v3, /device:TPU:0, one launch (start us, length us, event | category | flops | bytes accessed | tf_op | source)
XLA Modules:
  0.0 53.1 jit_solution(10731793519184223896)
XLA Ops:
  0.6 50.9 %shard_map.68 = (bf16[1,8]{1,0:T(2,128)(2,1)}, bf16[8,8192]{1,0:T(8,128)(2,1)}) custom-call(s32[1,8]{1,0:T(1,128)} %bitcast.4, s32[1,8]{1,0:T(1,128)} %bitcast.5, bf16[1,8]{1,0:T(2,128)(2,1)} %bitcast.6, bf16[8,8192]{1,0:T(8,128)(2,1)} %hidden_ref.1, bf16[1,8192,2048]{2,1,0:T(8,128)(2,1)} %w_hbm.1), custom_call_target="tpu_custom_call" | custom-call | tf_op jit(solution)/shard_map/pallas_call | solution.py:296
  51.5 1.6 %shard_map.69 = (bf16[1,8]{1,0:T(2,128)(2,1)}, bf16[8,8192]{1,0:T(8,128)(2,1)}) custom-call(bf16[1,8]{1,0:T(2,128)(2,1)} %get-tuple-element.6.loss_in, bf16[8,8192]{1,0:T(8,128)(2,1)} %get-tuple-element.7.grad_in), custom_call_target="tpu_custom_call" | custom-call | tf_op jit(solution)/shard_map/pallas_call | solution.py:341

commit v4 on v3

--- a/solution.py
+++ b/solution.py
@@ -43,14 +43,14 @@
     group = n_vocab * own
     columns = w_ref.shape[1]
 
-    def span(k):
+    def narrow_span(k):
         return pl.ds(pl.multiple_of(k * width, width), width)
 
     def wide_span(k):
         return pl.ds(pl.multiple_of(k * wide, wide), wide)
 
     def load_weight(k):
-        return pltpu.make_async_copy(w_hbm.at[0, span(k)], w_ref.at[span(k)], w_sem.at[k])
+        return pltpu.make_async_copy(w_hbm.at[0, narrow_span(k)], w_ref.at[narrow_span(k)], w_sem.at[k])
 
     for k in range(chunks):
         load_weight(k).start()
@@ -162,8 +162,8 @@
         for i in range(chunks // batches):
             j = k * (chunks // batches) + i
             load_weight(j).wait()
-            x = rows[:, :, span(j)].reshape(group, width)
-            logit_ref[...] += jnp.dot(x, w_ref[span(j), :], preferred_element_type=F32)
+            x = rows[:, :, narrow_span(j)].reshape(group, width)
+            logit_ref[...] += jnp.dot(x, w_ref[narrow_span(j), :], preferred_element_type=F32)
         return carry
 
     lax.fori_loop(0, batches, multiply, 0)
@@ -206,55 +206,55 @@
     give_back = jnp.where(give_back, 1.0, 0.0).astype(BF16)
 
     def back(k, carry):
-        @pl.when(k < chunks)
+        @pl.when(k < batches)
         def _():
             value = lax.dot_general(
-                w_ref[span(k), :], dlog_ref[...], (((1,), (1,)), ((), ())),
+                w_ref[wide_span(k), :], dlog_ref[...], (((1,), (1,)), ((), ())),
                 preferred_element_type=F32,
             )
-            part[k % 2] = value.T.reshape(2, n_chip, own, width)
-            pair_out[:, :, span(k)] = part[k % 2, 1 - core].astype(BF16)
-            remote(pair_out.at[:, :, span(k)], pair_in.at[:, :, span(k)],
+            part[k % 2] = value.T.reshape(2, n_chip, own, wide)
+            pair_out[:, :, wide_span(k)] = part[k % 2, 1 - core].astype(BF16)
+            remote(pair_out.at[:, :, wide_span(k)], pair_in.at[:, :, wide_span(k)],
                    pair_s, pair_r.at[k], partner).start()
 
-        @pl.when((k >= 1) & (k < chunks + 1))
+        @pl.when((k >= 1) & (k < batches + 1))
         def _():
             j = k - 1
-            whole(pair_in, n_chip, pair_s, pair_r.at[j], span(j)).wait_recv()
+            whole(pair_in, n_chip, pair_s, pair_r.at[j], wide_span(j)).wait_recv()
             for d in range(1, n_chip):
                 to = (chip + d) % n_chip
-                both = part[j % 2, core, to] + pair_in[to, :, span(j)].astype(F32)
-                sum_out[d, :, span(j)] = both.astype(BF16)
-                remote(sum_out.at[d, :, span(j)], sum_in.at[d, :, span(j)],
+                both = part[j % 2, core, to] + pair_in[to, :, wide_span(j)].astype(F32)
+                sum_out[d, :, wide_span(j)] = both.astype(BF16)
+                remote(sum_out.at[d, :, wide_span(j)], sum_in.at[d, :, wide_span(j)],
                        sum_s, sum_r.at[j], chip_peer(d)).start()
-            both = part[j % 2, core, chip] + pair_in[chip, :, span(j)].astype(F32)
-            sum_in[0, :, span(j)] = both.astype(BF16)
-
-        @pl.when((k >= 2) & (k < chunks + 2))
+            both = part[j % 2, core, chip] + pair_in[chip, :, wide_span(j)].astype(F32)
+            sum_in[0, :, wide_span(j)] = both.astype(BF16)
+
+        @pl.when((k >= 2) & (k < batches + 2))
         def _():
             j = k - 2
-            whole(sum_in, n_chip - 1, sum_s, sum_r.at[j], span(j)).wait_recv()
-            stage[:, span(j)] = jnp.sum(sum_in[:, :, span(j)].astype(F32), axis=0)
+            whole(sum_in, n_chip - 1, sum_s, sum_r.at[j], wide_span(j)).wait_recv()
+            stage[:, wide_span(j)] = jnp.sum(sum_in[:, :, wide_span(j)].astype(F32), axis=0)
             for d in range(n_head):
-                piece = stage[d * CAP : (d + 1) * CAP, span(j)].astype(BF16)
-                (back_out if d else back_in)[d, :, span(j)] = piece
+                piece = stage[d * CAP : (d + 1) * CAP, wide_span(j)].astype(BF16)
+                (back_out if d else back_in)[d, :, wide_span(j)] = piece
                 if d:
-                    remote(back_out.at[d, :, span(j)], back_in.at[d, :, span(j)],
+                    remote(back_out.at[d, :, wide_span(j)], back_in.at[d, :, wide_span(j)],
                            back_s, back_r.at[j], head_peer(-d)).start()
 
-        @pl.when(k >= 4)
-        def _():
-            j = k - 4
-            whole(back_in, n_head - 1, back_s, back_r.at[j], span(j)).wait_recv()
+        @pl.when(k >= 3)
+        def _():
+            j = k - 3
+            whole(back_in, n_head - 1, back_s, back_r.at[j], wide_span(j)).wait_recv()
             for d in range(n_head):
-                stage[d * CAP : (d + 1) * CAP, span(j)] = back_in[d, :, span(j)].astype(F32)
-            grad_ref[:, span(j)] = jnp.dot(
-                give_back, stage[:, span(j)].astype(BF16), preferred_element_type=F32
+                stage[d * CAP : (d + 1) * CAP, wide_span(j)] = back_in[d, :, wide_span(j)].astype(F32)
+            grad_ref[:, wide_span(j)] = jnp.dot(
+                give_back, stage[:, wide_span(j)].astype(BF16), preferred_element_type=F32
             ).astype(BF16)
 
         return carry
 
-    lax.fori_loop(0, chunks + 4, back, 0)
+    lax.fori_loop(0, batches + 3, back, 0)
 
     whole(loss_in, n_head - 1, loss_s, loss_r).wait_recv()
     loss = jnp.zeros((1, local), F32)
@@ -290,7 +290,6 @@
     n_chip = n_vocab // 2
     group = n_vocab * own
     chunks = CHUNKS
-    width = depth // chunks
     vmem = pl.BlockSpec(memory_space=pltpu.VMEM)
     dma = pltpu.SemaphoreType.DMA
     loss, grad = pl.pallas_call(
@@ -313,7 +312,7 @@
             pltpu.VMEM((group, columns), F32),
             pltpu.VMEM((group, columns), BF16),
             pltpu.VMEM((n_vocab, 8, group), F32),
-            pltpu.VMEM((2, 2, n_chip, own, width), F32),
+            pltpu.VMEM((2, 2, n_chip, own, depth // BATCHES), F32),
             pltpu.VMEM((n_chip, own, depth), BF16),
             pltpu.VMEM((n_chip, own, depth), BF16),
             pltpu.VMEM((n_chip, own, depth), BF16),
@@ -329,9 +328,9 @@
             dma, dma((BATCHES,)),
             dma, dma,
             dma, dma,
-            dma, dma((chunks,)),
-            dma, dma((chunks,)),
-            dma, dma((chunks,)),
+            dma, dma((BATCHES,)),
+            dma, dma((BATCHES,)),
+            dma, dma((BATCHES,)),
             dma, dma,
         ],
         compiler_params=pltpu.CompilerParams(

time: 53.2 us -> 49.2 us (0.925)
  Pallas kernels: 52.5 us -> 48.4 us
    pallas_call x1, Pallas kernels: 50.9 us -> 46.8 us  [per_device(): pl.pallas_call(functools.partial(kernel, n_head, n_vocab, chunks, BATCHES...]
where the time goes in v4:
time: 49.2 us; the launch traced here: 49.1 us
  Pallas kernels  48.4 us (98%)
  between operations  0.64 us (1%)
    pallas_call x1, Pallas kernels, per_device(): pl.pallas_call(functools.partial(kernel, n_head, n_vocab, chunks, BATCHES...  46.8 us
    pallas_call x1, Pallas kernels, per_device(): pl.pallas_call(hand_over, out_shape=(jax.ShapeDtypeStruct((1, local), BF1...  1.58 us

profile of v4, /device:TPU:0, one launch (start us, length us, event | category | flops | bytes accessed | tf_op | source)
XLA Modules:
  0.0 49.1 jit_solution(13378942170637594774)
XLA Ops:
  0.6 46.8 %shard_map.68 = (bf16[1,8]{1,0:T(2,128)(2,1)}, bf16[8,8192]{1,0:T(8,128)(2,1)}) custom-call(s32[1,8]{1,0:T(1,128)} %bitcast.4, s32[1,8]{1,0:T(1,128)} %bitcast.5, bf16[1,8]{1,0:T(2,128)(2,1)} %bitcast.6, bf16[8,8192]{1,0:T(8,128)(2,1)} %hidden_ref.1, bf16[1,8192,2048]{2,1,0:T(8,128)(2,1)} %w_hbm.1), custom_call_target="tpu_custom_call" | custom-call | tf_op jit(solution)/shard_map/pallas_call | solution.py:295
  47.5 1.6 %shard_map.69 = (bf16[1,8]{1,0:T(2,128)(2,1)}, bf16[8,8192]{1,0:T(8,128)(2,1)}) custom-call(bf16[1,8]{1,0:T(2,128)(2,1)} %get-tuple-element.6.loss_in, bf16[8,8192]{1,0:T(8,128)(2,1)} %get-tuple-element.7.grad_in), custom_call_target="tpu_custom_call" | custom-call | tf_op jit(solution)/shard_map/pallas_call | solution.py:340
